TPU v7x, 32 devices: a whole 2x2x4 slice. The times are simulated.
32 devices in a mesh: gx: 8 (over z, x), gy: 4 (over y, core).
Axes of the slice: x: 2, y: 2, z: 4, core: 2. Of those that a mesh axis runs over, the one named last changes fastest.
Arguments:
- orbitals: float32 [32, 64, 32, 128], P(None, 'gx', 'gy'), may hold values from -340 to 340
- potential: float32 [64, 32, 128], P('gx', 'gy'), may hold values from -3 to 1
Outputs:
- orthonormal: float32 [32, 64, 32, 128], P(None, 'gx', 'gy')
- rfactor: float32 [32, 32], replicated
All inputs are finite; a program needn't handle non-finite values.
Results may differ from a plain program's by a relative error of at most 0.0003.
Values sent between devices are 32-bit elements; how exact they have to be, the bound alone decides.
A program may use at most 128 MiB of HBM per device.

v0:
```python
import functools
import numpy as np
import jax
import jax.numpy as jnp
from jax import lax
from jax.experimental import pallas as pl
from jax.experimental.pallas import tpu as pltpu
from jax.sharding import PartitionSpec as P

DEGREE = 3
REACH = 6
stencil_weights = (
    -5369.0 / 1800.0,
    12.0 / 7.0,
    -15.0 / 56.0,
    10.0 / 189.0,
    -1.0 / 112.0,
    2.0 / 1925.0,
    -1.0 / 16632.0,
)
grid_spacing = 0.5
filter_low = 4.0
filter_high = 46.0
centre_shift = 0.5 * (filter_high + filter_low)
half_width = 0.5 * (filter_high - filter_low)
scale = -0.5 / grid_spacing**2 / half_width
side_weights = tuple(scale * w for w in stencil_weights)
MESH = pl.DeviceIdType.MESH


def circulant(size):
    matrix = np.zeros((size, size), np.float64)
    for offset in range(1, REACH + 1):
        for i in range(size):
            matrix[i, (i + offset) % size] += side_weights[offset]
            matrix[i, (i - offset) % size] += side_weights[offset]
    return matrix


def split_const(matrix):
    parts, rest = [], matrix
    for _ in range(3):
        part = rest.astype(jnp.bfloat16)
        parts.append(part)
        rest = rest - part.astype(np.float64)
    return parts


def split(value):
    high = value.astype(jnp.bfloat16)
    rest = value - high.astype(jnp.float32)
    mid = rest.astype(jnp.bfloat16)
    low = (rest - mid.astype(jnp.float32)).astype(jnp.bfloat16)
    return high, mid, low


def place(rows):
    gx, gy = lax.axis_index("gx"), lax.axis_index("gy")
    inner = lax.rem(gx, rows)
    return gx - inner, inner, gy


def steps_far_near(rows, n_gy):
    steps = sorted(range(rows), key=lambda j: -min(j, rows - j))
    pairs = [(j, d) for j in steps for d in range(n_gy) if (j, d) != (0, 0)]
    mixed = []
    while pairs:
        mixed.append(pairs.pop(0))
        if pairs:
            mixed.append(pairs.pop())
    return mixed


def greet(rows, n_gy):
    first, inner, gy = place(rows)
    barrier = pltpu.get_barrier_semaphore()
    for j in range(rows):
        for d in range(n_gy):
            if (j, d) != (0, 0):
                who = (first + lax.rem(inner + j, rows), lax.rem(gy + d, n_gy))
                pl.semaphore_signal(barrier, inc=1, device_id=who, device_id_type=MESH)
    pl.semaphore_wait(barrier, rows * n_gy - 1)


def spread(
    rows, n_gy, origin, orb, pot, field, allpot, send, recv, psend, precv, own, meanwhile=None
):
    bx, by = pot.shape[0], pot.shape[1]
    first, inner, gy = place(rows)
    gx_bits, gy_bits = rows.bit_length() - 1, n_gy.bit_length() - 1
    bits = gx_bits + gy_bits
    member = inner * n_gy + gy
    mine = [lax.rem(member // (1 << (bits - 1 - b)), 2) for b in range(bits)]
    brick = field.at[
        pl.ds(origin + inner * bx, bx), pl.ds(pl.multiple_of(gy * by, by), by)
    ]

    def region(done):
        index = [slice(None) if b in done else mine[b] for b in range(bits)]
        return allpot.at[tuple(index[:gx_bits]) + (slice(None),) + tuple(index[gx_bits:])]

    def hop(stage, bit, done):
        t = member + (1 << (bits - 1 - bit)) * (1 - 2 * mine[bit])
        return pltpu.make_async_remote_copy(
            region(done),
            region(done),
            psend.at[stage],
            precv.at[stage],
            device_id=(first + t // n_gy, lax.rem(t, n_gy)),
            device_id_type=MESH,
        )

    plain = list(range(bits))
    swapped = list(plain)
    if bits >= 3:
        swapped[bits - 3], swapped[bits - 2] = bits - 2, bits - 3
    odd = mine[bits - 1] == 1

    def on_hop(stage, act):
        if plain[: stage + 1] == swapped[: stage + 1] or stage == bits - 1:
            act(hop(stage, plain[stage], plain[:stage]))
        else:
            pl.when(jnp.logical_not(odd))(
                lambda: act(hop(stage, plain[stage], plain[:stage]))
            )
            pl.when(odd)(lambda: act(hop(stage, swapped[stage], swapped[:stage])))

    keep = pltpu.make_async_copy(orb.at[member], brick, own.at[0])
    keep_pot = pltpu.make_async_copy(pot, region([]), own.at[1])
    keep.start()
    keep_pot.start()
    greet(rows, n_gy)
    keep_pot.wait()

    order = steps_far_near(rows, n_gy)
    copies = []
    per = -(-len(order) // max(bits, 1))
    for b in range(bits):
        on_hop(b, lambda copy: copy.start())
        for j, d in order[b * per : (b + 1) * per]:
            tx, ty = lax.rem(inner + j, rows), lax.rem(gy + d, n_gy)
            copy = pltpu.make_async_remote_copy(
                orb.at[tx * n_gy + ty],
                brick,
                send.at[j * n_gy + d],
                recv.at[j * n_gy + d],
                device_id=(first + tx, ty),
                device_id_type=MESH,
            )
            copy.start()
            copies.append(copy)
        on_hop(b, lambda copy: copy.wait())
    if meanwhile is not None:
        meanwhile()
    for copy in copies:
        copy.wait()
    keep.wait()


def send_block(rows, n_gy, origin, j, field, out, send, recv, own):
    bx, by = out.shape[1], out.shape[2]
    first, inner, gy = place(rows)
    member = inner * n_gy + gy
    tx = lax.rem(inner + j, rows)
    copies = []
    for d in range(n_gy):
        ty = lax.rem(gy + d, n_gy)
        part = field.at[
            pl.ds(origin + tx * bx, bx), pl.ds(pl.multiple_of(ty * by, by), by)
        ]
        if (j, d) == (0, 0):
            copy = pltpu.make_async_copy(part, out.at[member], own)
        else:
            copy = pltpu.make_async_remote_copy(
                part,
                out.at[member],
                send.at[j * n_gy + d],
                recv.at[j * n_gy + d],
                device_id=(first + tx, ty),
                device_id_type=MESH,
            )
        copy.start()
        copies.append(copy)
    return copies


def block_order(rows):
    steps = sorted(range(1, rows), key=lambda j: -min(j, rows - j))
    mixed = []
    while steps:
        mixed.append(steps.pop(0))
        if steps:
            mixed.append(steps.pop())
    return mixed + [0]


def apply_planes(src, here, count, pot_planes, cz, cy, dst, there, prev):
    ny, nz = src.shape[1], src.shape[2]
    group = cy.shape[0] // ny
    centre = src[pl.ds(here, count)]
    acc = ((pot_planes - centre_shift) * (1.0 / half_width) + 3.0 * side_weights[0]) * centre
    high, mid, low = split(centre.reshape(count * ny, nz))
    lines = jnp.dot(
        jnp.concatenate([high, mid, low, high, mid, high], axis=1),
        cz[...],
        preferred_element_type=jnp.float32,
    )
    across = []
    for g in range(count // group):
        rows = slice(g * group * ny, (g + 1) * group * ny)
        h, m, l = high[rows], mid[rows], low[rows]
        across.append(
            jnp.dot(
                cy[...],
                jnp.concatenate([h, m, l, h, m, h], axis=0),
                preferred_element_type=jnp.float32,
            )
        )
    lines = lines + jnp.concatenate(across, axis=0)
    for offset in range(1, REACH + 1):
        acc += side_weights[offset] * (
            src[pl.ds(here + offset, count)] + src[pl.ds(here - offset, count)]
        )
    acc += lines.reshape(count, ny, nz)
    if prev is not None:
        acc = 2.0 * acc - prev[pl.ds(here, count)]
    dst[pl.ds(there, count)] = acc


def whole_kernel(
    rows, n_gy, orb, pot, cy_far, cz_far, out,
    cy_wide, cz_wide, cy, cz, first_buf, second_buf, allpot, send, recv, psend, precv, own, bsend, brecv,
):
    bx, ny, nz = pot.shape[0], first_buf.shape[1], first_buf.shape[2]
    extent = rows * bx
    gx_bits = rows.bit_length() - 1
    fetch = [
        pltpu.make_async_copy(cy_far, cy_wide, own.at[2]),
        pltpu.make_async_copy(cz_far, cz_wide, own.at[3]),
    ]
    for copy in fetch:
        copy.start()

    def fetched():
        for copy in fetch:
            copy.wait()
        cy[...] = cy_wide[...].astype(jnp.bfloat16)
        cz[...] = cz_wide[...].astype(jnp.bfloat16)

    spread(rows, n_gy, REACH, orb, pot, first_buf, allpot, send, recv, psend, precv, own,
           fetched)
    _, inner, _ = place(rows)

    def pot_block(block):
        index = tuple(lax.rem(block // (1 << (gx_bits - 1 - b)), 2) for b in range(gx_bits))
        return allpot[index].reshape(bx, ny, nz)

    def wrap(buf):
        buf[0:REACH] = buf[extent : extent + REACH]
        buf[extent + REACH : extent + 2 * REACH] = buf[REACH : 2 * REACH]

    bufs = (first_buf, second_buf)
    copies = []
    for step in range(1, DEGREE + 1):
        src, other = bufs[(step - 1) % 2], bufs[step % 2]
        wrap(src)
        prev = None if step == 1 else other
        if step < DEGREE:

            def body(block, carry, src=src, other=other, prev=prev):
                at = REACH + block * bx
                apply_planes(src, at, bx, pot_block(block), cz, cy, other, at, prev)
                return carry

            lax.fori_loop(0, rows, body, 0, unroll=True)
        else:
            for j in block_order(rows):
                block = lax.rem(inner + j, rows)
                at = REACH + block * bx
                apply_planes(src, at, bx, pot_block(block), cz, cy, other, at, prev)
                copies += send_block(
                    rows, n_gy, REACH, j, other, out, bsend, brecv, own.at[0]
                )
    for copy in copies:
        copy.wait()


def spread_kernel(rows, n_gy, orb, pot, field, allpot, send, recv, psend, precv, own):
    spread(rows, n_gy, 0, orb, pot, field, allpot, send, recv, psend, precv, own)


def return_kernel(rows, n_gy, field, out, send, recv, own):
    greet(rows, n_gy)
    copies = []
    for j in block_order(rows):
        copies += send_block(rows, n_gy, 0, j, field, out, send, recv, own)
    for copy in copies:
        copy.wait()


def filter_kernel(extent, field, pot, cy, cz, out, first_buf, second_buf):
    origin = REACH * DEGREE
    count = cy.shape[0] // field.shape[1]
    first_buf[...] = field[...]
    bufs = (first_buf, second_buf)
    for step in range(1, DEGREE + 1):
        src, other = bufs[(step - 1) % 2], bufs[step % 2]
        last = step == DEGREE
        margin = REACH * (DEGREE - step)
        prev = None if step == 1 else other
        dst, base = (out, 0) if last else (other, origin)

        def body(i, carry, src=src, dst=dst, base=base, prev=prev, margin=margin):
            at = i * count - margin
            planes = pot[pl.ds(origin + at, count)]
            apply_planes(src, origin + at, count, planes, cz, cy, dst, base + at, prev)
            return carry

        lax.fori_loop(0, (extent + 2 * margin) // count, body, 0)


def factor_kernel(
    n_gx, n_gy, cells, matrix, rfac, inverse, stack, ybuf, xbuf, ysend, yrecv, xsend, xrecv
):
    gx, gy = lax.axis_index("gx"), lax.axis_index("gy")
    norb = rfac.shape[0]
    nz = matrix.shape[1]
    lines = matrix.shape[0] // norb
    barrier = pltpu.get_barrier_semaphore()
    for k in range(1, n_gy):
        pl.semaphore_signal(
            barrier, inc=1, device_id=(gx, lax.rem(gy + k, n_gy)), device_id_type=MESH
        )
    for k in range(1, n_gx):
        pl.semaphore_signal(
            barrier, inc=1, device_id=(lax.rem(gx + k, n_gx), gy), device_id_type=MESH
        )

    for r in range(lines):
        for p, part in enumerate(split(matrix[pl.ds(r, norb, stride=lines)])):
            stack[p * norb : (p + 1) * norb, r * nz : (r + 1) * nz] = part
    square = lax.dot_general(
        stack[...], stack[...], (((1,), (1,)), ((), ())), preferred_element_type=jnp.float32
    )
    gram = None
    for p, q in ((2, 2), (1, 2), (2, 1), (0, 2), (2, 0), (1, 1), (0, 1), (1, 0), (0, 0)):
        term = square[p * norb : (p + 1) * norb, q * norb : (q + 1) * norb]
        gram = term if gram is None else gram + term
    pack = 128 // norb
    tall = norb // pack
    gram = gram / cells
    gram = jnp.concatenate([gram[i * tall : (i + 1) * tall] for i in range(pack)], axis=1)

    pl.semaphore_wait(barrier, n_gy + n_gx - 2)
    ybuf[gy] = gram
    copies = []
    for k in range(1, n_gy):
        copy = pltpu.make_async_remote_copy(
            ybuf.at[gy],
            ybuf.at[gy],
            ysend.at[k],
            yrecv.at[k],
            device_id=(gx, lax.rem(gy + k, n_gy)),
            device_id_type=MESH,
        )
        copy.start()
        copies.append(copy)
    for copy in copies:
        copy.wait()
    part = ybuf[0]
    for s in range(1, n_gy):
        part = part + ybuf[s]
    xbuf[gx] = part
    copies = []
    for k in range(1, n_gx):
        copy = pltpu.make_async_remote_copy(
            xbuf.at[gx],
            xbuf.at[gx],
            xsend.at[k],
            xrecv.at[k],
            device_id=(lax.rem(gx + k, n_gx), gy),
            device_id_type=MESH,
        )
        copy.start()
        copies.append(copy)
    for copy in copies:
        copy.wait()
    whole = xbuf[0]
    for s in range(1, n_gx):
        whole = whole + xbuf[s]

    row = lax.broadcasted_iota(jnp.int32, (norb, 128), 0)
    col = lax.broadcasted_iota(jnp.int32, (norb, 128), 1)
    whole = jnp.concatenate([whole[:, i * norb : (i + 1) * norb] for i in range(pack)], axis=0)
    whole = jnp.concatenate([whole, jnp.zeros((norb, 128 - norb), jnp.float32)], axis=1)
    table = jnp.where(col == row + norb, 1.0, whole)
    pivots = jnp.zeros((norb, 128), jnp.float32)
    for k in range(norb):
        pivot = table[k : k + 1, k : k + 1]
        pivots = jnp.where(row == k, pivot, pivots)
        ratio = jnp.where(row[:, :1] > k, table[:, k : k + 1] * (1.0 / pivot), 0.0)
        table = table - ratio * table[k : k + 1, :]
    table = table * lax.rsqrt(pivots)
    rfac[...] = jnp.where(row[:, :norb] <= col[:, :norb], table[:, :norb], 0.0)
    inverse[...] = table[:, norb : 2 * norb]


def mix_kernel(matrix, inverse, upper, out, rfac):
    rfac[...] = upper[...]
    norb = inverse.shape[0]
    lines = matrix.shape[0] // norb
    nz = matrix.shape[1]
    h, m, l = split(inverse[...])
    left = jnp.concatenate([h, h, h, m, m, l], axis=1)
    for r in range(0, lines, 2):
        both = jnp.concatenate(
            [matrix[pl.ds(r + i, norb, stride=lines)] for i in range(2)], axis=1
        )
        h, m, l = split(both)
        mixed = jnp.dot(
            left,
            jnp.concatenate([h, m, l, h, m, h], axis=0),
            preferred_element_type=jnp.float32,
        )
        for i in range(2):
            out[pl.ds(r + i, norb, stride=lines)] = mixed[:, i * nz : (i + 1) * nz]


def per_device(n_gx, n_gy, orbitals, potential):
    norb, bx, by, nz = orbitals.shape
    rows = norb // n_gy
    groups = n_gx // rows
    extent, ny = rows * bx, n_gy * by
    f32 = jnp.float32
    anywhere = pl.BlockSpec(memory_space=pltpu.HBM)
    vmem = pl.BlockSpec(memory_space=pltpu.VMEM)
    dma = pltpu.SemaphoreType.DMA
    gx_bits, gy_bits = rows.bit_length() - 1, n_gy.bit_length() - 1
    bits = gx_bits + gy_bits
    pot_shape = (2,) * gx_bits + (bx,) + (2,) * gy_bits + (by, nz)
    spread_sems = [dma((norb,)), dma((norb,)), dma((bits,)), dma((bits,)), dma((4,))]
    brick_shape = jax.ShapeDtypeStruct((norb, bx, by, nz), f32)

    yh, ym, yl = split_const(np.kron(np.eye(4), circulant(ny)))
    cy = jnp.asarray(np.concatenate([yh, yh, yh, ym, ym, yl], axis=1), f32)
    zh, zm, zl = split_const(circulant(nz))
    cz = jnp.asarray(np.concatenate([zh, zh, zh, zm, zm, zl], axis=0), f32)

    if groups == 1:
        planes = extent + 2 * REACH
        back = pl.pallas_call(
            functools.partial(whole_kernel, rows, n_gy),
            out_shape=brick_shape,
            in_specs=[anywhere] * 4,
            out_specs=vmem,
            scratch_shapes=[
                pltpu.VMEM(cy.shape, f32),
                pltpu.VMEM(cz.shape, f32),
                pltpu.VMEM(cy.shape, jnp.bfloat16),
                pltpu.VMEM(cz.shape, jnp.bfloat16),
                pltpu.VMEM((planes, ny, nz), f32),
                pltpu.VMEM((planes, ny, nz), f32),
                pltpu.VMEM(pot_shape, f32),
            ]
            + spread_sems
            + [dma((norb,)), dma((norb,))],
            compiler_params=pltpu.CompilerParams(
                collective_id=0, has_side_effects=True, vmem_limit_bytes=60 << 20
            ),
            name="spread_filter_return",
        )(orbitals, potential, cy, cz)
    else:
        field, allpot = pl.pallas_call(
            functools.partial(spread_kernel, rows, n_gy),
            out_shape=(
                jax.ShapeDtypeStruct((extent, ny, nz), f32),
                jax.ShapeDtypeStruct(pot_shape, f32),
            ),
            in_specs=[anywhere] * 2,
            out_specs=(anywhere, anywhere),
            scratch_shapes=spread_sems,
            compiler_params=pltpu.CompilerParams(collective_id=0, has_side_effects=True),
            name="spread",
        )(orbitals, potential)
        halo = REACH * DEGREE
        up = [(i, (i + rows) % n_gx) for i in range(n_gx)]
        down = [(t, s) for s, t in up]

        def widen(block):
            low = lax.ppermute(block[extent - halo :], "gx", up)
            high = lax.ppermute(block[:halo], "gx", down)
            return jnp.concatenate([low, block, high], axis=0)

        planes = extent + 2 * halo
        filtered = pl.pallas_call(
            functools.partial(filter_kernel, extent),
            out_shape=jax.ShapeDtypeStruct((extent, ny, nz), f32),
            in_specs=[vmem] * 4,
            out_specs=vmem,
            scratch_shapes=[pltpu.VMEM((planes, ny, nz), f32)] * 2,
            compiler_params=pltpu.CompilerParams(vmem_limit_bytes=24 << 20),
            name="filter",
        )(
            widen(field),
            widen(allpot.reshape(extent, ny, nz)),
            cy.astype(jnp.bfloat16),
            cz.astype(jnp.bfloat16),
        )
        back = pl.pallas_call(
            functools.partial(return_kernel, rows, n_gy),
            out_shape=brick_shape,
            in_specs=[anywhere],
            out_specs=anywhere,
            scratch_shapes=[dma((norb,)), dma((norb,)), dma],
            compiler_params=pltpu.CompilerParams(collective_id=1, has_side_effects=True),
            name="hand_back",
        )(filtered)

    matrix = back.reshape(norb * bx * by, nz)
    cells = float(bx * by * nz * n_gx * n_gy)
    upper, inverse = pl.pallas_call(
        functools.partial(factor_kernel, n_gx, n_gy, cells),
        out_shape=(jax.ShapeDtypeStruct((norb, norb), f32),) * 2,
        in_specs=[vmem],
        out_specs=(vmem, vmem),
        scratch_shapes=[
            pltpu.VMEM((3 * norb, bx * by * nz), jnp.bfloat16),
            pltpu.VMEM((n_gy, norb * norb // 128, 128), f32),
            pltpu.VMEM((n_gx, norb * norb // 128, 128), f32),
            dma((n_gy,)),
            dma((n_gy,)),
            dma((n_gx,)),
            dma((n_gx,)),
        ],
        compiler_params=pltpu.CompilerParams(
            collective_id=2, has_side_effects=True, vmem_limit_bytes=24 << 20
        ),
        name="factor",
    )(matrix)
    final, rfactor = pl.pallas_call(
        mix_kernel,
        out_shape=(
            jax.ShapeDtypeStruct(matrix.shape, f32),
            jax.ShapeDtypeStruct((norb, norb), f32),
        ),
        in_specs=[vmem] * 3,
        out_specs=(vmem, vmem),
        compiler_params=pltpu.CompilerParams(vmem_limit_bytes=24 << 20),
        name="mix",
    )(matrix, inverse, upper)
    return (final.reshape(orbitals.shape), rfactor)


def solution(mesh):
    return jax.shard_map(
        functools.partial(per_device, mesh.shape["gx"], mesh.shape["gy"]),
        mesh=mesh,
        in_specs=(P(None, "gx", "gy", None), P("gx", "gy", None)),
        out_specs=(P(None, "gx", "gy", None), P()),
        check_vma=False,
    )
```

profile of v0, /device:TPU:0, one launch (start us, length us, event | category | flops | bytes accessed | tf_op | source)
XLA Modules:
  0.0 84.2 jit_solution(1967387266994830513)
XLA Ops:
  0.6 65.5 %spread_filter_return.1 = f32[32,8,8,128]{3,2,1,0:T(8,128)} custom-call(f32[32,8,8,128]{3,2,1,0:T(8,128)} %orb.1, f32[8,8,128]{2,1,0:T(8,128)} %pot.1, f32[128,768]{1,0:T(8,128)} %constant.4.clone.cy_far, f32[768,128]{1,0:T(8,128)} %constant.5.clone.cz_far), custom_call_target="tpu_custom_call" | custom-call | tf_op jit(solution)/shard_map/spread_filter_return/pallas_call | solution.py:451
  66.2 0.0 copy-start
  66.2 1.2 %copy-done = f32[32,8,8,128]{3,2,1,0:T(8,128)S(1)} copy-done((f32[32,8,8,128]{3,2,1,0:T(8,128)S(1)}, f32[32,8,8,128]{3,2,1,0:T(8,128)}, u32[]{:S(2)}) %copy-start) | copy-done | bytes 1048600
  67.4 14.6 %factor.1 = (f32[32,32]{1,0:T(8,128)S(1)}, f32[32,32]{1,0:T(8,128)S(1)}) custom-call(f32[2048,128]{1,0:T(8,128)S(1)} %bitcast.2), custom_call_target="tpu_custom_call" | custom-call | tf_op jit(solution)/shard_map/factor/pallas_call | solution.py:521
  82.0 2.2 %mix.1 = (f32[2048,128]{1,0:T(8,128)}, f32[32,32]{1,0:T(8,128)}) custom-call(f32[2048,128]{1,0:T(8,128)S(1)} %bitcast.3, f32[32,32]{1,0:T(8,128)S(1)} %get-tuple-element.6.inverse, f32[32,32]{1,0:T(8,128)S(1)} %get-tuple-element.7.upper), custom_call_target="tpu_custom_call" | custom-call | tf_op jit(solution)/shard_map/mix/pallas_call | solution.py:540
Async XLA Ops:
  66.2 1.2 %copy-start = (f32[32,8,8,128]{3,2,1,0:T(8,128)S(1)}, f32[32,8,8,128]{3,2,1,0:T(8,128)}, u32[]{:S(2)}) copy-start(f32[32,8,8,128]{3,2,1,0:T(8,128)} %spread_filter_return.1) | copy-start | bytes 3145732
where the time goes:
time: 84.4 us; the launch traced here: 84.2 us
  Pallas kernels  82.3 us (98%)
  local copies, waits for them, and re-layouts  1.22 us (1%)
    pallas_call x1, Pallas kernels, per_device(): pl.pallas_call(functools.partial(whole_kernel, rows, n_gy), out_shape=bri...  65.5 us
    pallas_call x1, Pallas kernels, per_device(): pl.pallas_call(functools.partial(factor_kernel, n_gx, n_gy, cells), out_s...  14.6 us
    pallas_call x1, Pallas kernels, per_device(): pl.pallas_call(mix_kernel, out_shape=(jax.ShapeDtypeStruct(matrix.shape,...  2.21 us

commit v1 on v0

--- a/solution.py
+++ b/solution.py
@@ -196,27 +196,29 @@
 
 def apply_planes(src, here, count, pot_planes, cz, cy, dst, there, prev):
     ny, nz = src.shape[1], src.shape[2]
-    group = cy.shape[0] // ny
+    half = cy.shape[1] // 2
     centre = src[pl.ds(here, count)]
     acc = ((pot_planes - centre_shift) * (1.0 / half_width) + 3.0 * side_weights[0]) * centre
     high, mid, low = split(centre.reshape(count * ny, nz))
-    lines = jnp.dot(
-        jnp.concatenate([high, mid, low, high, mid, high], axis=1),
-        cz[...],
-        preferred_element_type=jnp.float32,
+
+    def dot(left, right):
+        return jnp.dot(left, right, preferred_element_type=jnp.float32)
+
+    def beside(value):
+        return jnp.concatenate(
+            [value[g : g + half] for g in range(0, count * ny, half)], axis=1
+        )
+
+    along = dot(jnp.concatenate([high, mid], axis=1), cz[:, : 2 * nz])
+    lines = along[:, :nz] + along[:, nz:]
+    lines = lines + dot(jnp.concatenate([low, high], axis=1), cz[:, 2 * nz :])
+    high, mid, low = beside(high), beside(mid), beside(low)
+    across = dot(cy[: 2 * half], jnp.concatenate([high, mid], axis=0))
+    across = across[:half] + across[half:]
+    across = across + dot(cy[2 * half :], jnp.concatenate([low, high], axis=0))
+    lines = lines + jnp.concatenate(
+        [across[:, g : g + nz] for g in range(0, across.shape[1], nz)], axis=0
     )
-    across = []
-    for g in range(count // group):
-        rows = slice(g * group * ny, (g + 1) * group * ny)
-        h, m, l = high[rows], mid[rows], low[rows]
-        across.append(
-            jnp.dot(
-                cy[...],
-                jnp.concatenate([h, m, l, h, m, h], axis=0),
-                preferred_element_type=jnp.float32,
-            )
-        )
-    lines = lines + jnp.concatenate(across, axis=0)
     for offset in range(1, REACH + 1):
         acc += side_weights[offset] * (
             src[pl.ds(here + offset, count)] + src[pl.ds(here - offset, count)]
@@ -228,7 +230,8 @@
 
 
 def whole_kernel(
-    rows, n_gy, orb, pot, cy_far, cz_far, out,
+    rows, n_gy, cells, orb, pot, cy_far, cz_far, out, rfac, inverse,
+    back, stack, ybuf, xbuf, ysend, yrecv, xsend, xrecv,
     cy_wide, cz_wide, cy, cz, first_buf, second_buf, allpot, send, recv, psend, precv, own, bsend, brecv,
 ):
     bx, ny, nz = pot.shape[0], first_buf.shape[1], first_buf.shape[2]
@@ -279,10 +282,17 @@
                 at = REACH + block * bx
                 apply_planes(src, at, bx, pot_block(block), cz, cy, other, at, prev)
                 copies += send_block(
-                    rows, n_gy, REACH, j, other, out, bsend, brecv, own.at[0]
+                    rows, n_gy, REACH, j, other, back, bsend, brecv, own.at[0]
                 )
     for copy in copies:
         copy.wait()
+    keep = pltpu.make_async_copy(back, out, own.at[0])
+    keep.start()
+    flat = back.reshape(back.shape[0] * back.shape[1] * back.shape[2], nz)
+    factor(
+        rows, n_gy, cells, flat, rfac, inverse, stack, ybuf, xbuf, ysend, yrecv, xsend, xrecv
+    )
+    keep.wait()
 
 
 def spread_kernel(rows, n_gy, orb, pot, field, allpot, send, recv, psend, precv, own):
@@ -300,7 +310,7 @@
 
 def filter_kernel(extent, field, pot, cy, cz, out, first_buf, second_buf):
     origin = REACH * DEGREE
-    count = cy.shape[0] // field.shape[1]
+    count = cy.shape[1] // 2 // field.shape[1]
     first_buf[...] = field[...]
     bufs = (first_buf, second_buf)
     for step in range(1, DEGREE + 1):
@@ -319,23 +329,32 @@
         lax.fori_loop(0, (extent + 2 * margin) // count, body, 0)
 
 
-def factor_kernel(
+def greet_lines(n_gx, n_gy):
+    gx, gy = lax.axis_index("gx"), lax.axis_index("gy")
+    barrier = pltpu.get_barrier_semaphore()
+    for k in range(1, n_gy):
+        pl.semaphore_signal(
+            barrier, inc=1, device_id=(gx, lax.rem(gy + k, n_gy)), device_id_type=MESH
+        )
+    for k in range(1, n_gx):
+        pl.semaphore_signal(
+            barrier, inc=1, device_id=(lax.rem(gx + k, n_gx), gy), device_id_type=MESH
+        )
+    pl.semaphore_wait(barrier, n_gy + n_gx - 2)
+
+
+def factor_kernel(n_gx, n_gy, cells, *refs):
+    greet_lines(n_gx, n_gy)
+    factor(n_gx, n_gy, cells, *refs)
+
+
+def factor(
     n_gx, n_gy, cells, matrix, rfac, inverse, stack, ybuf, xbuf, ysend, yrecv, xsend, xrecv
 ):
     gx, gy = lax.axis_index("gx"), lax.axis_index("gy")
     norb = rfac.shape[0]
     nz = matrix.shape[1]
     lines = matrix.shape[0] // norb
-    barrier = pltpu.get_barrier_semaphore()
-    for k in range(1, n_gy):
-        pl.semaphore_signal(
-            barrier, inc=1, device_id=(gx, lax.rem(gy + k, n_gy)), device_id_type=MESH
-        )
-    for k in range(1, n_gx):
-        pl.semaphore_signal(
-            barrier, inc=1, device_id=(lax.rem(gx + k, n_gx), gy), device_id_type=MESH
-        )
-
     for r in range(lines):
         for p, part in enumerate(split(matrix[pl.ds(r, norb, stride=lines)])):
             stack[p * norb : (p + 1) * norb, r * nz : (r + 1) * nz] = part
@@ -351,7 +370,6 @@
     gram = gram / cells
     gram = jnp.concatenate([gram[i * tall : (i + 1) * tall] for i in range(pack)], axis=1)
 
-    pl.semaphore_wait(barrier, n_gy + n_gx - 2)
     ybuf[gy] = gram
     copies = []
     for k in range(1, n_gy):
@@ -405,11 +423,10 @@
     inverse[...] = table[:, norb : 2 * norb]
 
 
-def mix_kernel(matrix, inverse, upper, out, rfac):
+def mix_kernel(bricks, inverse, upper, out, rfac):
+    norb, lines, nz = bricks.shape
     rfac[...] = upper[...]
-    norb = inverse.shape[0]
-    lines = matrix.shape[0] // norb
-    nz = matrix.shape[1]
+    matrix, mixed_rows = bricks.reshape(norb * lines, nz), out.reshape(norb * lines, nz)
     h, m, l = split(inverse[...])
     left = jnp.concatenate([h, h, h, m, m, l], axis=1)
     for r in range(0, lines, 2):
@@ -423,7 +440,7 @@
             preferred_element_type=jnp.float32,
         )
         for i in range(2):
-            out[pl.ds(r + i, norb, stride=lines)] = mixed[:, i * nz : (i + 1) * nz]
+            mixed_rows[pl.ds(r + i, norb, stride=lines)] = mixed[:, i * nz : (i + 1) * nz]
 
 
 def per_device(n_gx, n_gy, orbitals, potential):
@@ -442,18 +459,32 @@
     brick_shape = jax.ShapeDtypeStruct((norb, bx, by, nz), f32)
 
     yh, ym, yl = split_const(np.kron(np.eye(4), circulant(ny)))
-    cy = jnp.asarray(np.concatenate([yh, yh, yh, ym, ym, yl], axis=1), f32)
+    cy = jnp.asarray(np.block([[yh, yh], [ym, ym], [yh, yl]]), f32)
     zh, zm, zl = split_const(circulant(nz))
-    cz = jnp.asarray(np.concatenate([zh, zh, zh, zm, zm, zl], axis=0), f32)
+    cz = jnp.asarray(np.block([[zh, zm, zh], [zh, zm, zl]]), f32)
+
+    cells = float(bx * by * nz * n_gx * n_gy)
+    small = (jax.ShapeDtypeStruct((norb, norb), f32),) * 2
+    factor_scratch = [
+        pltpu.VMEM((3 * norb, bx * by * nz), jnp.bfloat16),
+        pltpu.VMEM((n_gy, norb * norb // 128, 128), f32),
+        pltpu.VMEM((n_gx, norb * norb // 128, 128), f32),
+        dma((n_gy,)),
+        dma((n_gy,)),
+        dma((n_gx,)),
+        dma((n_gx,)),
+    ]
 
     if groups == 1:
         planes = extent + 2 * REACH
-        back = pl.pallas_call(
-            functools.partial(whole_kernel, rows, n_gy),
-            out_shape=brick_shape,
+        back, upper, inverse = pl.pallas_call(
+            functools.partial(whole_kernel, rows, n_gy, cells),
+            out_shape=(brick_shape,) + small,
             in_specs=[anywhere] * 4,
-            out_specs=vmem,
-            scratch_shapes=[
+            out_specs=(anywhere, vmem, vmem),
+            scratch_shapes=[pltpu.VMEM(brick_shape.shape, f32)]
+            + factor_scratch
+            + [
                 pltpu.VMEM(cy.shape, f32),
                 pltpu.VMEM(cz.shape, f32),
                 pltpu.VMEM(cy.shape, jnp.bfloat16),
@@ -467,7 +498,7 @@
             compiler_params=pltpu.CompilerParams(
                 collective_id=0, has_side_effects=True, vmem_limit_bytes=60 << 20
             ),
-            name="spread_filter_return",
+            name="spread_filter_return_factor",
         )(orbitals, potential, cy, cz)
     else:
         field, allpot = pl.pallas_call(
@@ -516,38 +547,30 @@
             name="hand_back",
         )(filtered)
 
-    matrix = back.reshape(norb * bx * by, nz)
-    cells = float(bx * by * nz * n_gx * n_gy)
-    upper, inverse = pl.pallas_call(
-        functools.partial(factor_kernel, n_gx, n_gy, cells),
-        out_shape=(jax.ShapeDtypeStruct((norb, norb), f32),) * 2,
-        in_specs=[vmem],
-        out_specs=(vmem, vmem),
-        scratch_shapes=[
-            pltpu.VMEM((3 * norb, bx * by * nz), jnp.bfloat16),
-            pltpu.VMEM((n_gy, norb * norb // 128, 128), f32),
-            pltpu.VMEM((n_gx, norb * norb // 128, 128), f32),
-            dma((n_gy,)),
-            dma((n_gy,)),
-            dma((n_gx,)),
-            dma((n_gx,)),
-        ],
-        compiler_params=pltpu.CompilerParams(
-            collective_id=2, has_side_effects=True, vmem_limit_bytes=24 << 20
-        ),
-        name="factor",
-    )(matrix)
+        upper, inverse = pl.pallas_call(
+            functools.partial(factor_kernel, n_gx, n_gy, cells),
+            out_shape=small,
+            in_specs=[vmem],
+            out_specs=(vmem, vmem),
+            scratch_shapes=factor_scratch,
+            compiler_params=pltpu.CompilerParams(
+                collective_id=2, has_side_effects=True, vmem_limit_bytes=24 << 20
+            ),
+            name="factor",
+        )(back.reshape(norb * bx * by, nz))
+
+    piece = 2 * by
+    block = pl.BlockSpec((norb, piece, nz), lambda i: (0, i, 0))
+    square = pl.BlockSpec((norb, norb), lambda i: (0, 0))
     final, rfactor = pl.pallas_call(
         mix_kernel,
-        out_shape=(
-            jax.ShapeDtypeStruct(matrix.shape, f32),
-            jax.ShapeDtypeStruct((norb, norb), f32),
-        ),
-        in_specs=[vmem] * 3,
-        out_specs=(vmem, vmem),
-        compiler_params=pltpu.CompilerParams(vmem_limit_bytes=24 << 20),
+        grid=(bx * by // piece,),
+        out_shape=(jax.ShapeDtypeStruct((norb, bx * by, nz), f32), small[0]),
+        in_specs=[block, square, square],
+        out_specs=(block, square),
+        compiler_params=pltpu.CompilerParams(vmem_limit_bytes=60 << 20),
         name="mix",
-    )(matrix, inverse, upper)
+    )(back.reshape(norb, bx * by, nz), inverse, upper)
     return (final.reshape(orbitals.shape), rfactor)
 
 

time: 84.4 us -> 83 us (0.983)
  local copies, waits for them, and re-layouts: 1.22 us -> 0 us
    unnamed x2 -> x0, local copies, waits for them, and re-layouts: 1.22 us -> none
    pallas_call x3 -> x2, Pallas kernels: 82.3 us -> 82.1 us  [the longest x1 78.2 us: per_device(): pl.pallas_call(functools.partial(whole_kernel, rows, n_gy, cells), out_sh...]
where the time goes in v1:
time: 83 us; the launch traced here: 82.8 us
  Pallas kernels  82.1 us (99%)
    pallas_call x1, Pallas kernels, per_device(): pl.pallas_call(functools.partial(whole_kernel, rows, n_gy, cells), out_sh...  78.2 us
    pallas_call x1, Pallas kernels, per_device(): pl.pallas_call(mix_kernel, grid=(bx * by // piece,), out_shape=(jax.Shape...  4 us

profile of v1, /device:TPU:0, one launch (start us, length us, event | category | flops | bytes accessed | tf_op | source)
XLA Modules:
  0.0 82.8 jit_solution(1407370118778146096)
XLA Ops:
  0.6 78.2 %spread_filter_return_factor.1 = (f32[32,8,8,128]{3,2,1,0:T(8,128)}, f32[32,32]{1,0:T(8,128)}, f32[32,32]{1,0:T(8,128)}) custom-call(f32[32,8,8,128]{3,2,1,0:T(8,128)} %orb.1, f32[8,8,128]{2,1,0:T(8,128)} %pot.1, f32[384,256]{1,0:T(8,128)} %constant.4.clone.cy_far, f32[256,384]{1,0:T(8,128)} %constant.5.clone.cz_far), custom_call_target="tpu_custom_call" | custom-call | tf_op jit(solution)/shard_map/spread_filter_return_factor/pallas_call | solution.py:480
  78.8 4.0 %mix.1 = (f32[32,64,128]{2,1,0:T(8,128)}, f32[32,32]{1,0:T(8,128)}) custom-call(f32[32,64,128]{2,1,0:T(8,128)} %bitcast.2, f32[32,32]{1,0:T(8,128)} %get-tuple-element.8.inverse, f32[32,32]{1,0:T(8,128)} %get-tuple-element.9.upper), custom_call_target="tpu_custom_call" | custom-call | tf_op jit(solution)/shard_map/mix/pallas_call | solution.py:565
